TPU v7x, 512 devices: a whole 4x4x16 slice. The times are simulated.
512 devices in a mesh: mp: 2 (over core), tp: 8 (over z_lo), lat: 32 (over x, y, z_hi).
Axes of the slice: x: 4, y: 4, z: 16 (z_hi: 2, z_lo: 8; z = z_hi * 8 + z_lo), core: 2. Of those that a mesh axis runs over, the one named last changes fastest.
Arguments:
- resid_in: bfloat16 [2, 384, 3584], P('mp', 'lat'), may hold values from -6 to 6
- pre_gain: bfloat16 [2, 3584], P('mp'), may hold values from 0.25 to 1.75
- w_gate: bfloat16 [2, 14336, 3584], P('mp', 'lat', 'tp'), may hold values from -0.09375 to 0.09375
- w_up: bfloat16 [2, 14336, 3584], P('mp', 'lat', 'tp'), may hold values from -0.09375 to 0.09375
- w_down: bfloat16 [2, 14336, 3584], P('mp', 'lat', 'tp'), may hold values from -1 to 1
- post_gain: bfloat16 [2, 3584], P('mp', 'tp'), may hold values from 0.25 to 1.75
- enc_weight: bfloat16 [2, 3584, 32768], P('mp', 'tp', 'lat'), may hold values from -0.0625 to 0.0625
- enc_bias: bfloat16 [32768], P('lat'), may hold values from -3 to 3
- dec_weight: bfloat16 [2, 3584, 32768], P('mp', 'tp', 'lat'), may hold values from -0.03125 to 0.03125
- dec_bias: bfloat16 [2, 3584], P('mp', 'tp'), may hold values from -3 to 3
- prompt_of_row: int32 [384], replicated, may hold values from 0 to 95, never falling along the last dimension, each value on 1 to 8 neighbouring positions
- pad_mask: int32 [384], replicated, may hold values 0 or 1
- pair_ids: int32 [96], replicated, may hold values from 0 to 95, each once
Outputs:
- enc_grad: bfloat16 [2, 3584, 32768], P('mp', 'tp', 'lat')
- dec_grad: bfloat16 [2, 3584, 32768], P('mp', 'tp', 'lat')
Inputs may be any that keep to these rules, and one draw needn't show every extreme that they name: `prompt_of_row`: never falls from one row to the next; each of the 96 prompts has 1 to 8 rows, one exactly 8. `pair_ids`: each slot once; the prompts in slots 2k and 2k + 1 form pair k.
All inputs are finite; a program needn't handle non-finite values.
Results may differ from a plain program's by a relative error of at most 0.014.
Values may be sent and summed in bfloat16 or wider, within the bound.
A program may use at most 64 MiB of HBM per device.

v0:
```python
import jax
import jax.numpy as jnp
from jax import lax
from jax.sharding import PartitionSpec as P

norm_eps = 1e-06


def rms_scale(values):
    return lax.rsqrt(jnp.mean(values * values, axis=-1, keepdims=True) + norm_eps)


def row_weights(prompt_of_row, pad_mask, pair_ids):
    prompt_count = pair_ids.shape[0]
    pair_count = prompt_count // 2
    pair_of_prompt = pair_ids // 2
    in_prompt = prompt_of_row[:, None] == jnp.arange(prompt_count, dtype=jnp.int32)[None, :]
    pair_of_row = jnp.sum(jnp.where(in_prompt, pair_of_prompt[None, :], 0), axis=1)
    in_pair = pair_of_row[:, None] == jnp.arange(pair_count, dtype=jnp.int32)[None, :]
    valid = pad_mask.astype(jnp.float32)
    counts = jnp.sum(jnp.where(in_pair, valid[:, None], jnp.float32(0.0)), axis=0)
    inverse = 1.0 / jnp.maximum(counts, jnp.float32(1.0))
    return valid * jnp.sum(jnp.where(in_pair, inverse[None, :], jnp.float32(0.0)), axis=1)


def local(
    resid_in,
    pre_gain,
    w_gate,
    w_up,
    w_down,
    post_gain,
    enc_weight,
    enc_bias,
    dec_weight,
    dec_bias,
    prompt_of_row,
    pad_mask,
    pair_ids,
):
    own_inputs = resid_in[0]
    feat_width = own_inputs.shape[1]
    tp_count = lax.axis_size("tp")
    col_width = feat_width // tp_count
    col_first = lax.axis_index("tp") * col_width
    inputs_f = own_inputs.astype(jnp.float32)
    normed_own = (inputs_f * rms_scale(inputs_f) * pre_gain[0].astype(jnp.float32)[None, :]).astype(
        jnp.bfloat16
    )
    normed_cols = lax.dynamic_slice_in_dim(normed_own, col_first, col_width, 1)
    input_cols = lax.dynamic_slice_in_dim(own_inputs, col_first, col_width, 1)
    gain_out = post_gain[0].astype(jnp.float32)
    down_weight = w_down[0]
    normed, inputs_all = (
        lax.all_gather(normed_cols, "lat", axis=0, tiled=True),
        lax.all_gather(input_cols, "lat", axis=0, tiled=True),
    )
    contract_last = (((1,), (1,)), ((), ()))
    gate_part = lax.dot_general(
        normed, w_gate[0], contract_last, preferred_element_type=jnp.float32
    )
    up_part = lax.dot_general(normed, w_up[0], contract_last, preferred_element_type=jnp.float32)
    gate_out, upward = lax.psum((gate_part, up_part), "tp")
    hidden = (jax.nn.gelu(gate_out, approximate=True) * upward).astype(jnp.bfloat16)
    mixed_part = jnp.dot(hidden, down_weight, preferred_element_type=jnp.float32)
    mixed_sum = lax.psum(mixed_part, "lat")
    row_total = lax.psum(jnp.sum(mixed_sum * mixed_sum, axis=1), "tp")
    row_scale = lax.rsqrt(row_total / feat_width + norm_eps)
    resid = (
        inputs_all.astype(jnp.float32) + mixed_sum * row_scale[:, None] * gain_out[None, :]
    ).astype(jnp.bfloat16)
    enc_w = enc_weight[0]
    dec_w = dec_weight[0]
    model_index = lax.axis_index("mp")
    encoded = jnp.dot(resid, enc_w, preferred_element_type=jnp.float32)
    col_squares = jnp.sum(jnp.square(dec_w.astype(jnp.float32)), axis=0)
    model_slots = jnp.arange(2, dtype=jnp.int32)[:, None] == model_index
    norm_slots = jnp.where(model_slots, col_squares[None, :], jnp.float32(0.0))
    pre_sum, norm_sq = lax.psum((encoded, norm_slots), ("mp", "tp"))
    col_norms = jnp.sqrt(norm_sq + norm_eps)
    own_norm = jnp.sum(jnp.where(model_slots, col_norms, jnp.float32(0.0)), axis=0)
    norm_total = col_norms[0] + col_norms[1]
    pre_act = pre_sum + enc_bias.astype(jnp.float32)[None, :]
    active = jnp.maximum(pre_act, jnp.float32(0.0))
    features = (active * active).astype(jnp.bfloat16)
    weight_rows = row_weights(prompt_of_row, pad_mask, pair_ids)
    bias_cols = dec_bias[0].astype(jnp.float32)[None, :]
    recon_part = lax.dot_general(features, dec_w, contract_last, preferred_element_type=jnp.float32)
    recon = lax.psum(recon_part, "lat")
    recon_error = recon + bias_cols - resid.astype(jnp.float32)
    err_grad = (2.0 * weight_rows[:, None] * recon_error).astype(jnp.bfloat16)
    contract_rows = (((0,), (0,)), ((), ()))
    weighted = jnp.sum(weight_rows[:, None] * features.astype(jnp.float32), axis=0)
    direct = lax.dot_general(err_grad, features, contract_rows, preferred_element_type=jnp.float32)
    dec_grad = (direct + weighted[None, :] * dec_w.astype(jnp.float32) / own_norm[None, :]).astype(
        jnp.bfloat16
    )
    back_prop = jnp.dot(err_grad, dec_w, preferred_element_type=jnp.float32)
    feat_grad = lax.psum(back_prop, ("mp", "tp")) + weight_rows[:, None] * norm_total[None, :]
    pre_grad = (feat_grad * 2.0 * active).astype(jnp.bfloat16)
    enc_grad = lax.dot_general(
        resid, pre_grad, contract_rows, preferred_element_type=jnp.float32
    ).astype(jnp.bfloat16)
    return (enc_grad[None], dec_grad[None])


def solution(mesh):
    placed = (
        P("mp", "lat", None),
        P("mp", None),
        P("mp", "lat", "tp"),
        P("mp", "lat", "tp"),
        P("mp", "lat", "tp"),
        P("mp", "tp"),
        P("mp", "tp", "lat"),
        P("lat"),
        P("mp", "tp", "lat"),
        P("mp", "tp"),
        P(),
        P(),
        P(),
    )
    return jax.shard_map(
        local,
        mesh=mesh,
        in_specs=placed,
        out_specs=(P("mp", "tp", "lat"), P("mp", "tp", "lat")),
        check_vma=False,
    )
```

profile of v0, /device:TPU:1, one launch (start us, length us, event | category | flops | bytes accessed | tf_op | source)
XLA Modules:
  0.0 1972.4 jit_solution(16415838347782913750)
XLA Ops:
  7.2 0.0 copy-start
  7.2 0.0 copy-start.7
  7.2 0.0 all-reduce.15.cloned.1.call-start
  7.2 1.2 multiply_reduce_fusion.2
  8.4 0.9 bitcast_convert_fusion
  9.3 0.0 copy-start.8
  9.3 0.8 convert_reduce_fusion
  10.2 0.1 dynamic-slice.1
  10.2 0.1 fusion.40
  10.3 155.9 %all-gather.1 = bf16[32,12,448]{2,1,0:T(8,128)(2,1)S(1)} all-gather(bf16[1,12,448]{2,1,0:T(8,128)(2,1)S(1)} %fusion.40), channel_id=1, replica_groups=mesh['mp'=2,'tp'=8,'lat'=32] {'lat'}, dimensions={0}, use_global_device_ids=true | all-gather | bytes 354816 | tf_op jit(solution)/shard_map/all_gather | solution.py:55
  166.2 0.2 reshape.43
  166.4 0.0 copy-done.7
  166.4 1.3 fusion.29
  167.7 0.0 copy-done.8
  167.7 1.3 fusion.31
  168.9 0.0 all-reduce.15.cloned.1.call-update
  169.0 0.0 all-reduce.7.cloned.1.call-start
  169.0 130.5 %all-reduce.15.cloned.1.call-done = (f32[384,448]{0,1:T(8,128)}, f32[384,448]{0,1:T(8,128)}) async-done(((f32[384,448]{0,1:T(8,128)}, f32[384,448]{0,1:T(8,128)}), (f32[384,448]{0,1:T(8,128)}, f32[384,448]{0,1:T(8,128)})) %all-reduce.15.cloned.1.call-update) | async-done | bytes 1376272 | tf_op jit(solution)/shard_map/psum | solution.py:63
  299.5 0.0 copy-done.6
  299.5 2.7 fusion.27
  302.3 0.0 all-reduce.7.cloned.1.call-update
  302.3 0.0 all-reduce.9.cloned.1.call-start
  302.3 0.0 copy-done.11
  302.4 0.8 constant_dynamic-slice_fusion
  303.2 216.6 %all-gather = bf16[1,384,448]{2,0,1:T(2,128)(2,1)S(1)} all-gather(bf16[1,12,448]{2,0,1:T(2,128)(2,1)S(1)} %copy.21), channel_id=2, replica_groups=mesh['mp'=2,'tp'=8,'lat'=32] {'lat'}, dimensions={1}, use_global_device_ids=true | all-gather | bytes 354816 | tf_op jit(solution)/shard_map/all_gather | solution.py:56
  519.8 0.6 copy.20
  520.3 393.9 %all-reduce.7.cloned.1.call-done = f32[384,448]{0,1:T(8,128)} async-done(((f32[384,448]{0,1:T(8,128)}), f32[384,448]{0,1:T(8,128)}) %all-reduce.7.cloned.1.call-update) | async-done | bytes 688144 | tf_op jit(solution)/shard_map/psum | solution.py:66
  914.3 1.2 multiply_reduce_fusion.1
  915.5 23.6 %psum.59 = f32[384]{0:T(512)S(1)} all-reduce(f32[384]{0:T(512)S(1)} %multiply_reduce_fusion.1), channel_id=1, replica_groups=mesh['mp'=2,'tp'=8,'lat'=32] {'tp'}, use_global_device_ids=true, to_apply=%region_5.0 | all-reduce | flops 384 | bytes 3072 | tf_op jit(solution)/shard_map/psum | solution.py:67
  939.1 1.3 fusion.26
  940.4 0.0 copy-done
  940.4 0.0 copy-start.9
  940.4 0.0 copy-start.10
  940.4 0.0 copy-start.14
  940.4 0.0 copy-start.12
  940.4 1.7 fusion.10
  942.2 0.0 all-reduce.9.cloned.1.call-update
  942.2 0.0 copy-start.1
  942.2 0.0 all-reduce.11.cloned.1.call-start
  942.3 0.0 copy-done.14
  942.3 0.1 select_reduce_fusion
  942.4 0.1 select_reduce_fusion.2
  942.6 0.1 select_reduce_fusion.1
  942.7 230.8 %all-reduce.9.cloned.1.call-done = f32[384,1024]{1,0:T(8,128)} async-done(((f32[384,1024]{1,0:T(8,128)}), f32[384,1024]{1,0:T(8,128)}) %all-reduce.9.cloned.1.call-update) | async-done | bytes 1572880 | tf_op jit(solution)/shard_map/psum | solution.py:79
  1173.5 1.7 multiply_reduce_fusion
  1175.2 0.0 copy-start.4
  1175.2 0.0 copy-start.13
  1175.2 0.9 copy-done.4
  1176.0 1.5 fusion.8
  1177.6 0.0 all-reduce.11.cloned.1.call-update
  1177.6 0.0 all-reduce.13.cloned.1.call-start
  1177.7 555.9 %all-reduce.11.cloned.1.call-done = f32[384,448]{0,1:T(8,128)} async-done(((f32[384,448]{0,1:T(8,128)}), f32[384,448]{0,1:T(8,128)}) %all-reduce.11.cloned.1.call-update) | async-done | bytes 688144 | tf_op jit(solution)/shard_map/psum | solution.py:89
  1733.6 0.0 copy-done.3
  1733.6 1.3 multiply_convert_fusion.3
  1734.9 0.7 copy-done.5
  1735.6 1.7 fusion.6
  1737.3 0.0 all-reduce.13.cloned.1.call-update
  1737.4 0.2 fusion
  1737.6 0.1 broadcast_select_fusion
  1737.7 71.0 %psum.63 = f32[2,1024]{1,0:T(2,128)S(1)} all-reduce(f32[2,1024]{1,0:T(2,128)S(1)} %broadcast_select_fusion), channel_id=1, replica_groups=mesh['mp'=2,'tp'=8,'lat'=32] {'mp','tp'}, use_global_device_ids=true, to_apply=%region_13.14 | all-reduce | flops 2048 | bytes 16384 | tf_op jit(solution)/shard_map/psum | solution.py:79
  1808.7 0.1 select_reduce_fusion.3
  1808.8 2.9 fusion.5
  1811.8 150.9 %all-reduce.13.cloned.1.call-done = f32[384,1024]{1,0:T(8,128)} async-done(((f32[384,1024]{1,0:T(8,128)}), f32[384,1024]{1,0:T(8,128)}) %all-reduce.13.cloned.1.call-update) | async-done | bytes 1572880 | tf_op jit(solution)/shard_map/psum | solution.py:99
  1962.7 3.2 fusion.4
  (23 shorter events, 0.1 us)
Async XLA Ops:
  7.2 933.2 %copy-start = (bf16[1,448,1024]{2,1,0:T(8,128)(2,1)S(1)}, bf16[1,448,1024]{2,1,0:T(8,128)(2,1)}, u32[]{:S(2)}) copy-start(bf16[1,448,1024]{2,1,0:T(8,128)(2,1)} %param.19) | copy-start | bytes 2752516
  7.2 159.2 %copy-start.7 = (bf16[1,448,448]{2,1,0:T(8,128)(2,1)S(1)}, bf16[1,448,448]{2,1,0:T(8,128)(2,1)}, u32[]{:S(2)}) copy-start(bf16[1,448,448]{2,1,0:T(8,128)(2,1)} %param.16) | copy-start | bytes 1204228
  7.2 292.3 %all-reduce.15.cloned.1.call-start = ((), (), s32[]{:S(2)}) async-start(), calls=%async_computation.4 | async-start | bytes 2752512 | tf_op jit(solution)/shard_map/psum | solution.py:63
  9.3 158.4 %copy-start.8 = (bf16[1,448,448]{2,1,0:T(8,128)(2,1)S(1)}, bf16[1,448,448]{2,1,0:T(8,128)(2,1)}, u32[]{:S(2)}) copy-start(bf16[1,448,448]{2,1,0:T(8,128)(2,1)} %param.15) | copy-start | bytes 1204228
  167.7 131.9 %copy-start.6 = (bf16[1,448,448]{2,1,0:T(8,128)(2,1)S(1)}, bf16[1,448,448]{2,1,0:T(8,128)(2,1)}, u32[]{:S(2)}) copy-start(bf16[1,448,448]{2,1,0:T(8,128)(2,1)} %param.17) | copy-start | bytes 1204228
  169.0 745.3 %all-reduce.7.cloned.1.call-start = ((), (), s32[]{:S(2)}) async-start(), calls=%async_computation | async-start | bytes 1376256 | tf_op jit(solution)/shard_map/psum | solution.py:66
  299.5 2.8 copy-start.11
  302.3 871.2 %all-reduce.9.cloned.1.call-start = ((), (), s32[]{:S(2)}) async-start(), calls=%async_computation.1 | async-start | bytes 3145728 | tf_op jit(solution)/shard_map/psum | solution.py:79
  940.4 793.2 %copy-start.3 = (bf16[384,448]{0,1:T(8,128)(2,1)}, bf16[384,448]{0,1:T(8,128)(2,1)S(1)}, u32[]{:S(2)}) copy-start(bf16[384,448]{0,1:T(8,128)(2,1)S(1)} %fusion.26) | copy-start | bytes 1032196
  940.4 1.9 copy-start.9
  940.4 1.9 copy-start.10
  940.4 1.9 copy-start.14
  940.4 1.9 copy-start.12
  942.2 233.8 %copy-start.1 = (bf16[1,448,1024]{2,1,0:T(8,128)(2,1)S(1)}, bf16[1,448,1024]{2,1,0:T(8,128)(2,1)}, u32[]{:S(2)}) copy-start(bf16[1,448,1024]{2,1,0:T(8,128)(2,1)} %param.21) | copy-start | bytes 2752516
  942.2 791.4 %all-reduce.11.cloned.1.call-start = ((), (), s32[]{:S(2)}) async-start(), calls=%async_computation.2 | async-start | bytes 1376256 | tf_op jit(solution)/shard_map/psum | solution.py:89
  1175.2 0.9 copy-start.4
  1175.2 2.5 copy-start.13
  1177.6 785.1 %all-reduce.13.cloned.1.call-start = ((), (), s32[]{:S(2)}) async-start(), calls=%async_computation.3 | async-start | bytes 3145728 | tf_op jit(solution)/shard_map/psum | solution.py:99
  1734.9 0.7 copy-start.5
  1808.8 153.9 %copy-start.2 = (f32[384,1024]{1,0:T(8,128)S(1)}, f32[384,1024]{1,0:T(8,128)}, u32[]{:S(2)}) copy-start(f32[384,1024]{1,0:T(8,128)} %all-reduce.9.cloned.1.call-done) | copy-start | bytes 4718596
Sparse Core Ops, SparseCore 0:
  169.1 130.4 all-reduce.14
  303.3 610.9 all-reduce.6
  942.3 231.0 all-reduce.8
  1177.7 555.8 all-reduce.10
  1737.5 225.1 all-reduce.12
where the time goes:
time: 1970 us
  waiting for transfers between devices  1460 us (74%)
  blocking collectives  467 us (24%)
    psum x1, waiting for transfers between devices, local(): recon = lax.psum(recon_part, 'lat')  556 us
    psum x1, waiting for transfers between devices, local(): mixed_sum = lax.psum(mixed_part, 'lat')  394 us
    psum x1, waiting for transfers between devices, local(): pre_sum, norm_sq = lax.psum((encoded, norm_slots), ('mp', 'tp'))  231 us
    all_gather x1, blocking collectives, local(): lax.all_gather(input_cols, 'lat', axis=0, tiled=True)  217 us
    all_gather x1, blocking collectives, local(): lax.all_gather(normed_cols, 'lat', axis=0, tiled=True)  156 us
    psum x1, waiting for transfers between devices, local(): lax.psum(back_prop, ('mp', 'tp'))  151 us
    psum x1, waiting for transfers between devices, local(): gate_out, upward = lax.psum((gate_part, up_part), 'tp')  131 us
    psum x1, blocking collectives, local(): pre_sum, norm_sq = lax.psum((encoded, norm_slots), ('mp', 'tp'))  71 us
  transfers between devices with their start and end apart: 5, of which 5 were waited for; matrix products, arithmetic and copies ran while one was open for 0% of the time, Pallas kernels for 0%

commit v1 on v0

v1 whole, which is shorter than its diff:
```python
import functools

import jax
import jax.numpy as jnp
from jax import lax
from jax.experimental import pallas as pl
from jax.experimental.pallas import tpu as pltpu
from jax.sharding import PartitionSpec as P

MESH = pl.DeviceIdType.MESH
f32, bf16 = jnp.float32, jnp.bfloat16
EPS = 1e-06
NB = 3
ROWS = 384
R = ROWS // NB
RZ = R // 8
RX = R // 16
CW = 448
LW = 1024
HL = 512

LAST = (((1,), (1,)), ((), ()))
PLAIN = (((1,), (0,)), ((), ()))
FIRST = (((0,), (0,)), ((), ()))


def dot(a, b, dims=PLAIN):
    return lax.dot_general(a, b, dims, preferred_element_type=f32)


def merge(v, rows):
    return v.astype(f32).reshape(rows, v.shape[-1]).astype(bf16)


SCRATCH = {
    "payload": pltpu.VMEM((2, 12, 512), bf16),
    "own24": pltpu.VMEM((24, 512), f32),
    "nx": pltpu.VMEM((16, 24, 512), bf16),
    "xf": pltpu.VMEM((ROWS, 512), f32),
    "wgu": pltpu.VMEM((2 * CW, CW), bf16),
    "wrow": pltpu.VMEM((ROWS, 128), f32),
    "nsq": pltpu.VMEM((8, 1, LW), f32),
    "cn": pltpu.VMEM((2, 1, LW), f32),
    "pg": pltpu.VMEM((NB, 8, RZ, 2 * CW), bf16),
    "rg": pltpu.VMEM((NB, 8, RZ, 2 * CW), bf16),
    "hd": pltpu.VMEM((NB, 8, RZ, CW), bf16),
    "pm": pltpu.VMEM((2, NB, 16, RX, CW), bf16),
    "rm": pltpu.VMEM((2, NB, 16, RX, CW), bf16),
    "hs": pltpu.VMEM((2, NB, RX, CW), bf16),
    "hr": pltpu.VMEM((2, NB, RX, CW), bf16),
    "sq": pltpu.VMEM((NB, 8, RX, 128), f32),
    "rsd": pltpu.VMEM((NB, 16, RX, CW), bf16),
    "err": pltpu.VMEM((NB, 16, RX, CW), bf16),
    "ms": pltpu.VMEM((2, NB, R, HL), bf16),
    "mr": pltpu.VMEM((2, NB, R, HL), bf16),
    "pe": pltpu.VMEM((2, NB, 8, RZ, HL), bf16),
    "re": pltpu.VMEM((2, NB, 8, RZ, HL), bf16),
    "act": pltpu.VMEM((NB, RZ, HL), f32),
    "fe": pltpu.VMEM((NB, 2, 8, RZ, HL), bf16),
    "pd": pltpu.VMEM((NB, 2, 8, RZ, HL), bf16),
    "sem": pltpu.SemaphoreType.DMA((2, 200 * NB + 40)),
}


def kernel(*refs):
    (x_ref, pre_ref, wg_ref, wu_ref, wd_ref, post_ref, ew_ref, eb_ref, dw_ref, db_ref,
     prompt_ref, pad_ref, ids_ref, eg_ref, dg_ref) = refs[:15]
    s = dict(zip(SCRATCH, refs[15:]))
    sem = s["sem"]
    m, i, lat = lax.axis_index("mp"), lax.axis_index("tp"), lax.axis_index("lat")
    q, h = lax.div(lat, 2), lax.rem(lat, 2)
    to_z = [{"tp": lax.rem(i + k, 8)} for k in range(1, 8)]
    to_q = [lax.rem(q + k, 16) for k in range(1, 16)]
    to_xy = [{"lat": 2 * p + h} for p in to_q]
    to_h = {"lat": 2 * q + 1 - h}
    to_m = {"mp": 1 - m}

    gate = pltpu.get_barrier_semaphore()
    everyone = to_z + to_xy + [to_h, to_m]
    for d in everyone:
        pl.semaphore_signal(gate, inc=1, device_id=d, device_id_type=MESH)

    used, sends = [0], []

    def send(src, dst, where):
        n = used[0]
        used[0] += 1
        c = pltpu.make_async_remote_copy(
            src_ref=src, dst_ref=dst, send_sem=sem.at[0, n], recv_sem=sem.at[1, n],
            device_id=where, device_id_type=MESH)
        c.start()
        sends.append(c)
        return c

    def wait(copies):
        for c in copies:
            c.wait_recv()

    def z_scatter(src, dst):
        return [send(src.at[lax.rem(i + k, 8)], dst.at[k], to_z[k - 1]) for k in range(1, 8)]

    def z_gather(ref):
        return [send(ref.at[i], ref.at[i], to_z[k - 1]) for k in range(1, 8)]

    def xy_scatter(src, dst):
        return [send(src.at[to_q[k - 1]], dst.at[k], to_xy[k - 1]) for k in range(1, 16)]

    def xy_gather(ref):
        return [send(ref.at[q], ref.at[q], to_xy[k - 1]) for k in range(1, 16)]

    def total(own, ref, count):
        acc = own.astype(f32)
        for k in range(1, count):
            acc = acc + ref[k].astype(f32)
        return acc

    x = x_ref[0].astype(f32)
    scale = lax.rsqrt(jnp.sum(x * x, axis=1, keepdims=True) / (8 * CW) + EPS)
    p0 = scale.astype(bf16).astype(f32)
    p1 = (scale - p0).astype(bf16).astype(f32)
    p2 = scale - p0 - p1
    cols = jnp.zeros((12, CW), f32)
    gain_in = jnp.zeros((1, CW), f32)
    pre = pre_ref[...].astype(f32)
    for c in range(8):
        cols = jnp.where(i == c, x[:, c * CW:(c + 1) * CW], cols)
        gain_in = jnp.where(i == c, pre[:, c * CW:(c + 1) * CW], gain_in)
    payload = jnp.concatenate([cols, jnp.zeros((12, 64), f32)], axis=1)
    lane = lax.broadcasted_iota(jnp.int32, (12, 512), 1)
    payload = jnp.where(lane == CW, p0, jnp.where(lane == CW + 1, p1, jnp.where(lane == CW + 2, p2, payload)))
    s["payload"][h] = payload.astype(bf16)

    dw = dw_ref[0].astype(f32)
    s["nsq"][i] = jnp.sum(dw * dw, axis=0, keepdims=True)

    pl.semaphore_wait(gate, len(everyone))

    wait([send(s["payload"].at[h], s["payload"].at[h], to_h)])
    s["own24"][0:12] = s["payload"][0].astype(f32)
    s["own24"][12:24] = s["payload"][1].astype(f32)
    s["nx"][q] = s["own24"][...].astype(bf16)
    x_copies = xy_gather(s["nx"])
    norm_copies = z_gather(s["nsq"])

    def column(v):
        return jnp.broadcast_to(v, (128, v.shape[1])).T[:, :1]

    prompt = column(prompt_ref[...])
    valid = column(pad_ref[...].astype(f32))
    in_prompt = prompt == lax.broadcasted_iota(jnp.int32, (ROWS, 96), 1)
    pair_of_prompt = lax.shift_right_logical(ids_ref[...], 1).astype(f32)
    pair = jnp.sum(jnp.where(in_prompt, pair_of_prompt, 0.0), axis=1, keepdims=True)
    in_pair = pair == lax.broadcasted_iota(jnp.int32, (ROWS, 48), 1).astype(f32)
    counts = jnp.sum(jnp.where(in_pair, valid, 0.0), axis=0, keepdims=True)
    inverse = 1.0 / jnp.maximum(counts, 1.0)
    wrow = valid * jnp.sum(jnp.where(in_pair, inverse, 0.0), axis=1, keepdims=True)
    s["wrow"][...] = jnp.broadcast_to(wrow, (ROWS, 128))
    s["wgu"][0:CW] = wg_ref[0]
    s["wgu"][CW:2 * CW] = wu_ref[0]

    post = post_ref[...].astype(f32)
    dbias = db_ref[...].astype(f32)
    half = pl.ds(pl.multiple_of(m * HL, HL), HL)
    other = pl.ds(pl.multiple_of((1 - m) * HL, HL), HL)

    wait(x_copies)
    s["xf"][...] = s["nx"][...].astype(f32).reshape(ROWS, 512)

    def mp_and_tp_sum(b, t, left, weight):
        s["ms"][t, b] = dot(left, weight[0, :, other]).astype(bf16)
        c = send(s["ms"].at[t, b], s["mr"].at[t, b], to_m)
        mine = dot(left, weight[0, :, half])
        c.wait_recv()
        both = mine + s["mr"][t, b].astype(f32)
        s["pe"][t, b] = both.reshape(8, RZ, HL).astype(bf16)
        return z_scatter(s["pe"].at[t, b], s["re"].at[t, b])

    def lat_sum(b, t, part):
        s["pm"][t, b] = part.reshape(16, RX, CW).astype(bf16)
        return xy_scatter(s["pm"].at[t, b], s["rm"].at[t, b])

    def block(b):
        rows = slice(b * R, (b + 1) * R)
        own_x = pl.ds(pl.multiple_of(b * R + q * RX, 8), RX)
        own_z = pl.ds(pl.multiple_of(b * R + i * RZ, 8), RZ)
        xb = s["xf"][rows]
        row_scale = xb[:, CW:CW + 1] + xb[:, CW + 1:CW + 2] + xb[:, CW + 2:CW + 3]
        normed = (xb[:, :CW] * row_scale * gain_in).astype(bf16)
        s["pg"][b] = dot(normed, s["wgu"][...], LAST).reshape(8, RZ, 2 * CW).astype(bf16)
        c = z_scatter(s["pg"].at[b], s["rg"].at[b])
        yield
        wait(c)
        both = total(s["pg"][b, i], s["rg"].at[b], 8)
        g, u = both[:, :CW], both[:, CW:]
        s["hd"][b, i] = (0.5 * g * (1.0 + jnp.tanh(0.7978845608028654 * (g + 0.044715 * g * g * g))) * u).astype(bf16)
        c = z_gather(s["hd"].at[b])
        yield
        wait(c)
        c = lat_sum(b, 0, dot(merge(s["hd"][b], R), wd_ref[0]))
        yield
        wait(c)
        s["hs"][0, b] = total(s["pm"][0, b, q], s["rm"].at[0, b], 16).astype(bf16)
        c = [send(s["hs"].at[0, b], s["hr"].at[0, b], to_h)]
        yield
        wait(c)
        mixed = s["hs"][0, b].astype(f32) + s["hr"][0, b].astype(f32)
        s["sq"][b, i] = jnp.broadcast_to(jnp.sum(mixed * mixed, axis=1, keepdims=True), (RX, 128))
        c = z_gather(s["sq"].at[b])
        yield
        wait(c)
        square = s["sq"][b, 0]
        for k in range(1, 8):
            square = square + s["sq"][b, k]
        out_scale = lax.rsqrt(square[:, :1] / (8 * CW) + EPS)
        s["rsd"][b, q] = (s["xf"][own_x, :][:, :CW] + mixed * out_scale * post).astype(bf16)
        c = xy_gather(s["rsd"].at[b])
        yield
        wait(c)
        c = mp_and_tp_sum(b, 0, merge(s["rsd"][b], R), ew_ref)
        yield
        wait(c)
        pre_act = total(s["pe"][0, b, i], s["re"].at[0, b], 8) + eb_ref[:, half].astype(f32)
        active = jnp.maximum(pre_act, 0.0)
        s["act"][b] = active
        s["fe"][b, m, i] = (active * active).astype(bf16)
        c = z_gather(s["fe"].at[b, m])
        yield
        wait(c)
        c = [send(s["fe"].at[b, m], s["fe"].at[b, m], to_m)]
        yield
        wait(c)
        recon = dot(merge(s["fe"][b, 0], R), dw_ref[0, :, :HL], LAST)
        recon = recon + dot(merge(s["fe"][b, 1], R), dw_ref[0, :, HL:], LAST)
        c = lat_sum(b, 1, recon)
        yield
        wait(c)
        s["hs"][1, b] = total(s["pm"][1, b, q], s["rm"].at[1, b], 16).astype(bf16)
        c = [send(s["hs"].at[1, b], s["hr"].at[1, b], to_h)]
        yield
        wait(c)
        error = s["hs"][1, b].astype(f32) + s["hr"][1, b].astype(f32) + dbias - s["rsd"][b, q].astype(f32)
        s["err"][b, q] = (2.0 * s["wrow"][own_x, :][:, :1] * error).astype(bf16)
        c = xy_gather(s["err"].at[b])
        yield
        wait(c)
        c = mp_and_tp_sum(b, 1, merge(s["err"][b], R), dw_ref)
        yield
        wait(c)
        norm_total = s["cn"][0, :, half] + s["cn"][1, :, half]
        grad = total(s["pe"][1, b, i], s["re"].at[1, b], 8) + s["wrow"][own_z, :][:, :1] * norm_total
        s["pd"][b, m, i] = (grad * 2.0 * s["act"][b]).astype(bf16)
        c = z_gather(s["pd"].at[b, m])
        yield
        wait(c)
        c = [send(s["pd"].at[b, m], s["pd"].at[b, m], to_m)]
        yield
        wait(c)

    running = [block(b) for b in range(NB)]
    phase = 0
    while running:
        running = [g for g in running if next(g, True) is None]
        phase += 1
        if phase == 2:
            wait(norm_copies)
            squares = s["nsq"][0]
            for k in range(1, 8):
                squares = squares + s["nsq"][k]
            s["cn"][m] = jnp.sqrt(squares + EPS)
            cn_copy = send(s["cn"].at[m], s["cn"].at[m], to_m)
        if phase == 3:
            cn_copy.wait_recv()
        if phase == 14:
            err = merge(s["err"][...], ROWS)
            own_norm = s["cn"][m]
            for p in range(2):
                at = slice(p * HL, (p + 1) * HL)
                feats = s["fe"][:, p].astype(f32).reshape(ROWS, HL)
                weighted = jnp.sum(s["wrow"][:, :1] * feats, axis=0, keepdims=True)
                direct = dot(err, feats.astype(bf16), FIRST)
                dg_ref[0, :, at] = (
                    direct + weighted * dw_ref[0, :, at].astype(f32) / own_norm[:, at]).astype(bf16)

    resid = merge(s["rsd"][...], ROWS)
    for p in range(2):
        at = slice(p * HL, (p + 1) * HL)
        eg_ref[0, :, at] = dot(resid, merge(s["pd"][:, p], ROWS), FIRST).astype(bf16)
    for c in sends:
        c.wait_send()


def local(*args):
    args = list(args)
    for n in (7, 10, 11, 12):
        args[n] = args[n][None]
    vmem = pl.BlockSpec(memory_space=pltpu.VMEM)
    out = jax.ShapeDtypeStruct((1, CW, LW), bf16)
    return pl.pallas_call(
        kernel,
        out_shape=(out, out),
        in_specs=[vmem] * 13,
        out_specs=(vmem, vmem),
        scratch_shapes=list(SCRATCH.values()),
        compiler_params=pltpu.CompilerParams(
            collective_id=1, has_side_effects=True, vmem_limit_bytes=56 << 20),
        cost_estimate=pl.CostEstimate(flops=2300000000, bytes_accessed=7000000, transcendentals=100000),
    )(*args)


def solution(mesh):
    placed = (
        P("mp", "lat", None),
        P("mp", None),
        P("mp", "lat", "tp"),
        P("mp", "lat", "tp"),
        P("mp", "lat", "tp"),
        P("mp", "tp"),
        P("mp", "tp", "lat"),
        P("lat"),
        P("mp", "tp", "lat"),
        P("mp", "tp"),
        P(),
        P(),
        P(),
    )
    return jax.shard_map(
        local,
        mesh=mesh,
        in_specs=placed,
        out_specs=(P("mp", "tp", "lat"), P("mp", "tp", "lat")),
        check_vma=False,
    )
```

time: 1970 us -> 215 us (0.11)
  waiting for transfers between devices: 1460 us -> 0 us
  blocking collectives: 467 us -> 0 us
  Pallas kernels: 0 us -> 209 us
    psum x5 -> x0, waiting for transfers between devices: 1460 us -> none  [the longest x1 556 us: local(): recon = lax.psum(recon_part, 'lat')]
    all_gather x2 -> x0, blocking collectives: 372 us -> none  [the longest x1 217 us: local(): lax.all_gather(input_cols, 'lat', axis=0, tiled=True)]
    pallas_call x0 -> x1, Pallas kernels: none -> 209 us  [local(): pl.pallas_call(kernel, out_shape=(out, out), in_specs=[vmem] * 13, out_sp...]
    psum x2 -> x0, blocking collectives: 94.7 us -> none  [the longest x1 71 us: local(): pre_sum, norm_sq = lax.psum((encoded, norm_slots), ('mp', 'tp'))]
  transfers between devices with their start and end apart: 5 -> 0, of which waited for: 5 -> 0; matrix products, arithmetic and copies ran while one was open for 0% -> 0% of each run, Pallas kernels for 0% -> 0%
where the time goes in v1:
time: 215 us
  Pallas kernels  209 us (97%)
  local copies, waits for them, and re-layouts  5.7 us (3%)
    pallas_call x1, Pallas kernels, local(): pl.pallas_call(kernel, out_shape=(out, out), in_specs=[vmem] * 13, out_sp...  209 us

profile of v1, /device:TPU:1, one launch (start us, length us, event | category | flops | bytes accessed | tf_op | source)
XLA Modules:
  0.0 215.1 jit_solution(837827092033008951)
XLA Ops:
  0.6 0.0 copy-start.2
  0.6 1.3 broadcast_in_dim.13.refs_10_
  1.9 0.0 copy-done.2
  1.9 0.0 copy-start.1
  1.9 0.6 broadcast_in_dim.14.refs_11_
  2.5 0.1 copy-done.1
  2.6 0.6 broadcast_in_dim.12.refs_7_
  3.2 208.7 %shard_map.140 = (bf16[1,448,1024]{2,1,0:T(8,128)(2,1)}, bf16[1,448,1024]{2,1,0:T(8,128)(2,1)}) custom-call(bf16[1,12,3584]{2,1,0:T(8,128)(2,1)} %refs_0_.1, bf16[1,3584]{1,0:T(2,128)(2,1)} %refs_1_.1, bf16[1,448,448]{2,1,0:T(8,128)(2,1)} %refs_2_.1, bf16[1,448,448]{2,1,0:T(8,128)(2,1)} %refs_3_.1, bf16[1,448,448]{2,1,0:T(8,128)(2,1)} %refs_4_.1, ...), custom_call_target="tpu_custom_call" | custom-call | flops 2300000000 | bytes 7000000 | tf_op jit(solution)/shard_map/pallas_call | solution.py:298
  211.9 0.0 copy-start
  211.9 2.2 %copy.17 = bf16[1,448,1024]{2,1,0:T(8,128)(2,1)} copy(bf16[1,448,1024]{2,1,0:T(8,128)(2,1)} %get-tuple-element.4) | data formatting | bytes 1835008
  214.2 0.0 copy-done
  214.2 0.9 copy.18
Async XLA Ops:
  0.6 1.3 copy-start.2
  1.9 0.7 copy-start.1
  211.9 2.3 %copy-start = (bf16[1,448,1024]{2,1,0:T(8,128)(2,1)S(1)}, bf16[1,448,1024]{2,1,0:T(8,128)(2,1)}, u32[]{:S(2)}) copy-start(bf16[1,448,1024]{2,1,0:T(8,128)(2,1)} %get-tuple-element.5) | copy-start | bytes 2752516

commit v2 on v1

--- a/solution.py
+++ b/solution.py
@@ -12,6 +12,7 @@
 EPS = 1e-06
 NB = 3
 ROWS = 384
+LAG = 0
 R = ROWS // NB
 RZ = R // 8
 RX = R // 16
@@ -58,14 +59,21 @@
     "act": pltpu.VMEM((NB, RZ, HL), f32),
     "fe": pltpu.VMEM((NB, 2, 8, RZ, HL), bf16),
     "pd": pltpu.VMEM((NB, 2, 8, RZ, HL), bf16),
+    "wd": pltpu.VMEM((CW, CW), bf16),
+    "ew": pltpu.VMEM((CW, LW), bf16),
+    "dw": pltpu.VMEM((CW, LW), bf16),
+    "eg": pltpu.VMEM((CW, LW), bf16),
+    "dg": pltpu.VMEM((CW, LW), bf16),
+    "load": pltpu.SemaphoreType.DMA((8,)),
     "sem": pltpu.SemaphoreType.DMA((2, 200 * NB + 40)),
 }
 
 
 def kernel(*refs):
-    (x_ref, pre_ref, wg_ref, wu_ref, wd_ref, post_ref, ew_ref, eb_ref, dw_ref, db_ref,
-     prompt_ref, pad_ref, ids_ref, eg_ref, dg_ref) = refs[:15]
+    (x_ref, pre_ref, wg_hbm, wu_hbm, wd_hbm, post_ref, ew_hbm, eb_ref, dw_hbm, db_ref,
+     prompt_ref, pad_ref, ids_ref, eg_hbm, dg_hbm) = refs[:15]
     s = dict(zip(SCRATCH, refs[15:]))
+    wd_ref, ew_ref, dw_ref, eg_ref, dg_ref = s["wd"], s["ew"], s["dw"], s["eg"], s["dg"]
     sem = s["sem"]
     m, i, lat = lax.axis_index("mp"), lax.axis_index("tp"), lax.axis_index("lat")
     q, h = lax.div(lat, 2), lax.rem(lat, 2)
@@ -80,6 +88,15 @@
     for d in everyone:
         pl.semaphore_signal(gate, inc=1, device_id=d, device_id_type=MESH)
 
+    def local_copy(src, dst, n):
+        c = pltpu.make_async_copy(src, dst, s["load"].at[n])
+        c.start()
+        return c
+
+    load_d = local_copy(dw_hbm.at[0], dw_ref, 0)
+    load_g = [local_copy(wg_hbm.at[0], s["wgu"].at[pl.ds(0, CW)], 1),
+              local_copy(wu_hbm.at[0], s["wgu"].at[pl.ds(CW, CW)], 2)]
+    load_w = [local_copy(wd_hbm.at[0], wd_ref, 3), local_copy(ew_hbm.at[0], ew_ref, 4)]
     used, sends = [0], []
 
     def send(src, dst, where):
@@ -96,11 +113,40 @@
         for c in copies:
             c.wait_recv()
 
+    side, place = lax.div(i, 4), lax.rem(i, 4)
+    mates = [lax.rem(place + k, 4) for k in range(1, 4)]
+    to_mate = [{"tp": 4 * side + p} for p in mates]
+    across = lax.rem(i + 4, 8)
+    to_across = {"tp": across}
+
     def z_scatter(src, dst):
-        return [send(src.at[lax.rem(i + k, 8)], dst.at[k], to_z[k - 1]) for k in range(1, 8)]
+        far = [send(src.at[4 - 4 * side + p], dst.at[k], to_mate[k - 1]) for k, p in enumerate(mates, 1)]
+        near = [send(src.at[4 * side + p], dst.at[4 + k], to_mate[k - 1]) for k, p in enumerate(mates, 1)]
+        yield
+        wait(far)
+        src[across] = (src[across].astype(f32) + dst[1].astype(f32)
+                       + dst[2].astype(f32) + dst[3].astype(f32)).astype(bf16)
+        last = send(src.at[across], dst.at[4], to_across)
+        yield
+        wait(near + [last])
 
     def z_gather(ref):
+        first = send(ref.at[i], ref.at[i], to_across)
+        near = [send(ref.at[i], ref.at[i], d) for d in to_mate]
+        yield
+        wait([first])
+        far = [send(ref.at[across], ref.at[across], d) for d in to_mate]
+        yield
+        wait(near + far)
+
+    def z_share(ref):
         return [send(ref.at[i], ref.at[i], to_z[k - 1]) for k in range(1, 8)]
+
+    def z_total(own, ref):
+        acc = own.astype(f32)
+        for k in range(4, 8):
+            acc = acc + ref[k].astype(f32)
+        return acc
 
     def xy_scatter(src, dst):
         return [send(src.at[to_q[k - 1]], dst.at[k], to_xy[k - 1]) for k in range(1, 16)]
@@ -130,17 +176,18 @@
     payload = jnp.where(lane == CW, p0, jnp.where(lane == CW + 1, p1, jnp.where(lane == CW + 2, p2, payload)))
     s["payload"][h] = payload.astype(bf16)
 
-    dw = dw_ref[0].astype(f32)
+    pl.semaphore_wait(gate, len(everyone))
+
+    first = send(s["payload"].at[h], s["payload"].at[h], to_h)
+    load_d.wait()
+    dw = dw_ref[...].astype(f32)
     s["nsq"][i] = jnp.sum(dw * dw, axis=0, keepdims=True)
-
-    pl.semaphore_wait(gate, len(everyone))
-
-    wait([send(s["payload"].at[h], s["payload"].at[h], to_h)])
+    wait([first])
     s["own24"][0:12] = s["payload"][0].astype(f32)
     s["own24"][12:24] = s["payload"][1].astype(f32)
     s["nx"][q] = s["own24"][...].astype(bf16)
     x_copies = xy_gather(s["nx"])
-    norm_copies = z_gather(s["nsq"])
+    norm_copies = z_share(s["nsq"])
 
     def column(v):
         return jnp.broadcast_to(v, (128, v.shape[1])).T[:, :1]
@@ -155,25 +202,25 @@
     inverse = 1.0 / jnp.maximum(counts, 1.0)
     wrow = valid * jnp.sum(jnp.where(in_pair, inverse, 0.0), axis=1, keepdims=True)
     s["wrow"][...] = jnp.broadcast_to(wrow, (ROWS, 128))
-    s["wgu"][0:CW] = wg_ref[0]
-    s["wgu"][CW:2 * CW] = wu_ref[0]
 
     post = post_ref[...].astype(f32)
     dbias = db_ref[...].astype(f32)
     half = pl.ds(pl.multiple_of(m * HL, HL), HL)
     other = pl.ds(pl.multiple_of((1 - m) * HL, HL), HL)
 
+    for c in load_g + load_w:
+        c.wait()
     wait(x_copies)
     s["xf"][...] = s["nx"][...].astype(f32).reshape(ROWS, 512)
 
     def mp_and_tp_sum(b, t, left, weight):
-        s["ms"][t, b] = dot(left, weight[0, :, other]).astype(bf16)
+        s["ms"][t, b] = dot(left, weight[:, other]).astype(bf16)
         c = send(s["ms"].at[t, b], s["mr"].at[t, b], to_m)
-        mine = dot(left, weight[0, :, half])
+        mine = dot(left, weight[:, half])
         c.wait_recv()
         both = mine + s["mr"][t, b].astype(f32)
         s["pe"][t, b] = both.reshape(8, RZ, HL).astype(bf16)
-        return z_scatter(s["pe"].at[t, b], s["re"].at[t, b])
+        yield from z_scatter(s["pe"].at[t, b], s["re"].at[t, b])
 
     def lat_sum(b, t, part):
         s["pm"][t, b] = part.reshape(16, RX, CW).astype(bf16)
@@ -187,16 +234,12 @@
         row_scale = xb[:, CW:CW + 1] + xb[:, CW + 1:CW + 2] + xb[:, CW + 2:CW + 3]
         normed = (xb[:, :CW] * row_scale * gain_in).astype(bf16)
         s["pg"][b] = dot(normed, s["wgu"][...], LAST).reshape(8, RZ, 2 * CW).astype(bf16)
-        c = z_scatter(s["pg"].at[b], s["rg"].at[b])
-        yield
-        wait(c)
-        both = total(s["pg"][b, i], s["rg"].at[b], 8)
+        yield from z_scatter(s["pg"].at[b], s["rg"].at[b])
+        both = z_total(s["pg"][b, i], s["rg"].at[b])
         g, u = both[:, :CW], both[:, CW:]
         s["hd"][b, i] = (0.5 * g * (1.0 + jnp.tanh(0.7978845608028654 * (g + 0.044715 * g * g * g))) * u).astype(bf16)
-        c = z_gather(s["hd"].at[b])
-        yield
-        wait(c)
-        c = lat_sum(b, 0, dot(merge(s["hd"][b], R), wd_ref[0]))
+        yield from z_gather(s["hd"].at[b])
+        c = lat_sum(b, 0, dot(merge(s["hd"][b], R), wd_ref[...]))
         yield
         wait(c)
         s["hs"][0, b] = total(s["pm"][0, b, q], s["rm"].at[0, b], 16).astype(bf16)
@@ -205,7 +248,7 @@
         wait(c)
         mixed = s["hs"][0, b].astype(f32) + s["hr"][0, b].astype(f32)
         s["sq"][b, i] = jnp.broadcast_to(jnp.sum(mixed * mixed, axis=1, keepdims=True), (RX, 128))
-        c = z_gather(s["sq"].at[b])
+        c = z_share(s["sq"].at[b])
         yield
         wait(c)
         square = s["sq"][b, 0]
@@ -216,21 +259,17 @@
         c = xy_gather(s["rsd"].at[b])
         yield
         wait(c)
-        c = mp_and_tp_sum(b, 0, merge(s["rsd"][b], R), ew_ref)
-        yield
-        wait(c)
-        pre_act = total(s["pe"][0, b, i], s["re"].at[0, b], 8) + eb_ref[:, half].astype(f32)
+        yield from mp_and_tp_sum(b, 0, merge(s["rsd"][b], R), ew_ref)
+        pre_act = z_total(s["pe"][0, b, i], s["re"].at[0, b]) + eb_ref[:, half].astype(f32)
         active = jnp.maximum(pre_act, 0.0)
         s["act"][b] = active
         s["fe"][b, m, i] = (active * active).astype(bf16)
-        c = z_gather(s["fe"].at[b, m])
-        yield
-        wait(c)
+        yield from z_gather(s["fe"].at[b, m])
         c = [send(s["fe"].at[b, m], s["fe"].at[b, m], to_m)]
         yield
         wait(c)
-        recon = dot(merge(s["fe"][b, 0], R), dw_ref[0, :, :HL], LAST)
-        recon = recon + dot(merge(s["fe"][b, 1], R), dw_ref[0, :, HL:], LAST)
+        recon = dot(merge(s["fe"][b, 0], R), dw_ref[:, :HL], LAST)
+        recon = recon + dot(merge(s["fe"][b, 1], R), dw_ref[:, HL:], LAST)
         c = lat_sum(b, 1, recon)
         yield
         wait(c)
@@ -243,23 +282,22 @@
         c = xy_gather(s["err"].at[b])
         yield
         wait(c)
-        c = mp_and_tp_sum(b, 1, merge(s["err"][b], R), dw_ref)
-        yield
-        wait(c)
+        known.append(b)
+        yield from mp_and_tp_sum(b, 1, merge(s["err"][b], R), dw_ref)
         norm_total = s["cn"][0, :, half] + s["cn"][1, :, half]
-        grad = total(s["pe"][1, b, i], s["re"].at[1, b], 8) + s["wrow"][own_z, :][:, :1] * norm_total
+        grad = z_total(s["pe"][1, b, i], s["re"].at[1, b]) + s["wrow"][own_z, :][:, :1] * norm_total
         s["pd"][b, m, i] = (grad * 2.0 * s["act"][b]).astype(bf16)
-        c = z_gather(s["pd"].at[b, m])
-        yield
-        wait(c)
+        yield from z_gather(s["pd"].at[b, m])
         c = [send(s["pd"].at[b, m], s["pd"].at[b, m], to_m)]
         yield
         wait(c)
 
-    running = [block(b) for b in range(NB)]
+    out_copies = []
+    known = []
+    running = [(b, block(b)) for b in range(NB)]
     phase = 0
     while running:
-        running = [g for g in running if next(g, True) is None]
+        running = [(b, g) for b, g in running if phase < b * LAG or next(g, True) is None]
         phase += 1
         if phase == 2:
             wait(norm_copies)
@@ -270,7 +308,8 @@
             cn_copy = send(s["cn"].at[m], s["cn"].at[m], to_m)
         if phase == 3:
             cn_copy.wait_recv()
-        if phase == 14:
+        if len(known) == NB:
+            known.append(NB)
             err = merge(s["err"][...], ROWS)
             own_norm = s["cn"][m]
             for p in range(2):
@@ -278,15 +317,19 @@
                 feats = s["fe"][:, p].astype(f32).reshape(ROWS, HL)
                 weighted = jnp.sum(s["wrow"][:, :1] * feats, axis=0, keepdims=True)
                 direct = dot(err, feats.astype(bf16), FIRST)
-                dg_ref[0, :, at] = (
-                    direct + weighted * dw_ref[0, :, at].astype(f32) / own_norm[:, at]).astype(bf16)
+                dg_ref[:, at] = (
+                    direct + weighted * dw_ref[:, at].astype(f32) / own_norm[:, at]).astype(bf16)
+            out_copies.append(local_copy(dg_ref, dg_hbm.at[0], 5))
 
     resid = merge(s["rsd"][...], ROWS)
     for p in range(2):
         at = slice(p * HL, (p + 1) * HL)
-        eg_ref[0, :, at] = dot(resid, merge(s["pd"][:, p], ROWS), FIRST).astype(bf16)
+        eg_ref[:, at] = dot(resid, merge(s["pd"][:, p], ROWS), FIRST).astype(bf16)
+        out_copies.append(local_copy(eg_ref.at[:, at], eg_hbm.at[0, :, at], 6 + p))
     for c in sends:
         c.wait_send()
+    for c in out_copies:
+        c.wait()
 
 
 def local(*args):
@@ -294,12 +337,13 @@
     for n in (7, 10, 11, 12):
         args[n] = args[n][None]
     vmem = pl.BlockSpec(memory_space=pltpu.VMEM)
+    any_ = pl.BlockSpec(memory_space=pl.ANY)
     out = jax.ShapeDtypeStruct((1, CW, LW), bf16)
     return pl.pallas_call(
         kernel,
         out_shape=(out, out),
-        in_specs=[vmem] * 13,
-        out_specs=(vmem, vmem),
+        in_specs=[any_ if n in (2, 3, 4, 6, 8) else vmem for n in range(13)],
+        out_specs=(any_, any_),
         scratch_shapes=list(SCRATCH.values()),
         compiler_params=pltpu.CompilerParams(
             collective_id=1, has_side_effects=True, vmem_limit_bytes=56 << 20),

time: 215 us -> 178 us (0.83)
  Pallas kernels: 209 us -> 172 us
    pallas_call x1, Pallas kernels: 209 us -> 172 us  [local(): pl.pallas_call(kernel, out_shape=(out, out), in_specs=[any_ if n in (2, 3...]
where the time goes in v2:
time: 178 us
  Pallas kernels  172 us (97%)
  local copies, waits for them, and re-layouts  5.7 us (3%)
    pallas_call x1, Pallas kernels, local(): pl.pallas_call(kernel, out_shape=(out, out), in_specs=[any_ if n in (2, 3...  172 us

profile of v2, /device:TPU:1, one launch (start us, length us, event | category | flops | bytes accessed | tf_op | source)
XLA Modules:
  0.0 177.9 jit_solution(4587265084970208821)
XLA Ops:
  0.6 0.0 copy-start.2
  0.6 1.3 broadcast_in_dim.13.refs_10_
  1.9 0.0 copy-done.2
  1.9 0.0 copy-start.1
  1.9 0.6 broadcast_in_dim.14.refs_11_
  2.5 0.1 copy-done.1
  2.6 0.6 broadcast_in_dim.12.refs_7_
  3.2 171.6 %shard_map.140 = (bf16[1,448,1024]{2,1,0:T(8,128)(2,1)}, bf16[1,448,1024]{2,1,0:T(8,128)(2,1)}) custom-call(bf16[1,12,3584]{2,1,0:T(8,128)(2,1)} %refs_0_.1, bf16[1,3584]{1,0:T(2,128)(2,1)} %refs_1_.1, bf16[1,448,448]{2,1,0:T(8,128)(2,1)} %refs_2_.1, bf16[1,448,448]{2,1,0:T(8,128)(2,1)} %refs_3_.1, bf16[1,448,448]{2,1,0:T(8,128)(2,1)} %refs_4_.1, ...), custom_call_target="tpu_custom_call" | custom-call | flops 2300000000 | bytes 7000000 | tf_op jit(solution)/shard_map/pallas_call | solution.py:342
  174.7 0.0 copy-start
  174.7 2.2 %copy.17 = bf16[1,448,1024]{2,1,0:T(8,128)(2,1)} copy(bf16[1,448,1024]{2,1,0:T(8,128)(2,1)} %get-tuple-element.4) | data formatting | bytes 1835008
  177.0 0.0 copy-done
  177.0 0.9 copy.18
Async XLA Ops:
  0.6 1.3 copy-start.2
  1.9 0.7 copy-start.1
  174.7 2.3 %copy-start = (bf16[1,448,1024]{2,1,0:T(8,128)(2,1)S(1)}, bf16[1,448,1024]{2,1,0:T(8,128)(2,1)}, u32[]{:S(2)}) copy-start(bf16[1,448,1024]{2,1,0:T(8,128)(2,1)} %get-tuple-element.5) | copy-start | bytes 2752516

commit v3 on v2

--- a/solution.py
+++ b/solution.py
@@ -12,7 +12,6 @@
 EPS = 1e-06
 NB = 3
 ROWS = 384
-LAG = 0
 R = ROWS // NB
 RZ = R // 8
 RX = R // 16
@@ -64,8 +63,9 @@
     "dw": pltpu.VMEM((CW, LW), bf16),
     "eg": pltpu.VMEM((CW, LW), bf16),
     "dg": pltpu.VMEM((CW, LW), bf16),
+    "eb": pltpu.VMEM((1, LW), f32),
     "load": pltpu.SemaphoreType.DMA((8,)),
-    "sem": pltpu.SemaphoreType.DMA((2, 200 * NB + 40)),
+    "sem": pltpu.SemaphoreType.DMA((2, 32 * NB + 4)),
 }
 
 
@@ -99,18 +99,21 @@
     load_w = [local_copy(wd_hbm.at[0], wd_ref, 3), local_copy(ew_hbm.at[0], ew_ref, 4)]
     used, sends = [0], []
 
-    def send(src, dst, where):
+    def link(n, src, dst, where):
+        return pltpu.make_async_remote_copy(
+            src_ref=src, dst_ref=dst, send_sem=sem.at[0, n], recv_sem=sem.at[1, n],
+            device_id=where, device_id_type=MESH)
+
+    def send(copies, whole):
         n = used[0]
         used[0] += 1
-        c = pltpu.make_async_remote_copy(
-            src_ref=src, dst_ref=dst, send_sem=sem.at[0, n], recv_sem=sem.at[1, n],
-            device_id=where, device_id_type=MESH)
-        c.start()
-        sends.append(c)
-        return c
-
-    def wait(copies):
-        for c in copies:
+        for src, dst, where in copies:
+            link(n, src, dst, where).start()
+        sends.append(link(n, whole, whole, to_m))
+        return sends[-1]
+
+    def wait(*groups):
+        for c in groups:
             c.wait_recv()
 
     side, place = lax.div(i, 4), lax.rem(i, 4)
@@ -120,27 +123,29 @@
     to_across = {"tp": across}
 
     def z_scatter(src, dst):
-        far = [send(src.at[4 - 4 * side + p], dst.at[k], to_mate[k - 1]) for k, p in enumerate(mates, 1)]
-        near = [send(src.at[4 * side + p], dst.at[4 + k], to_mate[k - 1]) for k, p in enumerate(mates, 1)]
+        far = send([(src.at[4 - 4 * side + p], dst.at[k], to_mate[k - 1])
+                    for k, p in enumerate(mates, 1)], dst.at[pl.ds(1, 3)])
+        near = send([(src.at[4 * side + p], dst.at[4 + k], to_mate[k - 1])
+                     for k, p in enumerate(mates, 1)], dst.at[pl.ds(5, 3)])
         yield
         wait(far)
         src[across] = (src[across].astype(f32) + dst[1].astype(f32)
                        + dst[2].astype(f32) + dst[3].astype(f32)).astype(bf16)
-        last = send(src.at[across], dst.at[4], to_across)
-        yield
-        wait(near + [last])
+        last = send([(src.at[across], dst.at[4], to_across)], dst.at[4])
+        yield
+        wait(near, last)
 
     def z_gather(ref):
-        first = send(ref.at[i], ref.at[i], to_across)
-        near = [send(ref.at[i], ref.at[i], d) for d in to_mate]
-        yield
-        wait([first])
-        far = [send(ref.at[across], ref.at[across], d) for d in to_mate]
-        yield
-        wait(near + far)
+        first = send([(ref.at[i], ref.at[i], to_across)], ref.at[0])
+        near = send([(ref.at[i], ref.at[i], d) for d in to_mate], ref.at[pl.ds(0, 3)])
+        yield
+        wait(first)
+        far = send([(ref.at[across], ref.at[across], d) for d in to_mate], ref.at[pl.ds(0, 3)])
+        yield
+        wait(near, far)
 
     def z_share(ref):
-        return [send(ref.at[i], ref.at[i], to_z[k - 1]) for k in range(1, 8)]
+        return send([(ref.at[i], ref.at[i], d) for d in to_z], ref.at[pl.ds(0, 7)])
 
     def z_total(own, ref):
         acc = own.astype(f32)
@@ -149,10 +154,11 @@
         return acc
 
     def xy_scatter(src, dst):
-        return [send(src.at[to_q[k - 1]], dst.at[k], to_xy[k - 1]) for k in range(1, 16)]
+        return send([(src.at[to_q[k - 1]], dst.at[k], to_xy[k - 1]) for k in range(1, 16)],
+                    dst.at[pl.ds(1, 15)])
 
     def xy_gather(ref):
-        return [send(ref.at[q], ref.at[q], to_xy[k - 1]) for k in range(1, 16)]
+        return send([(ref.at[q], ref.at[q], d) for d in to_xy], ref.at[pl.ds(0, 15)])
 
     def total(own, ref, count):
         acc = own.astype(f32)
@@ -178,11 +184,11 @@
 
     pl.semaphore_wait(gate, len(everyone))
 
-    first = send(s["payload"].at[h], s["payload"].at[h], to_h)
+    first = send([(s["payload"].at[h], s["payload"].at[h], to_h)], s["payload"].at[0])
     load_d.wait()
     dw = dw_ref[...].astype(f32)
     s["nsq"][i] = jnp.sum(dw * dw, axis=0, keepdims=True)
-    wait([first])
+    wait(first)
     s["own24"][0:12] = s["payload"][0].astype(f32)
     s["own24"][12:24] = s["payload"][1].astype(f32)
     s["nx"][q] = s["own24"][...].astype(bf16)
@@ -192,10 +198,10 @@
     def column(v):
         return jnp.broadcast_to(v, (128, v.shape[1])).T[:, :1]
 
-    prompt = column(prompt_ref[...])
-    valid = column(pad_ref[...].astype(f32))
+    prompt = column(prompt_ref[...].reshape(1, ROWS))
+    valid = column(pad_ref[...].reshape(1, ROWS).astype(f32))
     in_prompt = prompt == lax.broadcasted_iota(jnp.int32, (ROWS, 96), 1)
-    pair_of_prompt = lax.shift_right_logical(ids_ref[...], 1).astype(f32)
+    pair_of_prompt = lax.shift_right_logical(ids_ref[...].reshape(1, 96), 1).astype(f32)
     pair = jnp.sum(jnp.where(in_prompt, pair_of_prompt, 0.0), axis=1, keepdims=True)
     in_pair = pair == lax.broadcasted_iota(jnp.int32, (ROWS, 48), 1).astype(f32)
     counts = jnp.sum(jnp.where(in_pair, valid, 0.0), axis=0, keepdims=True)
@@ -203,6 +209,7 @@
     wrow = valid * jnp.sum(jnp.where(in_pair, inverse, 0.0), axis=1, keepdims=True)
     s["wrow"][...] = jnp.broadcast_to(wrow, (ROWS, 128))
 
+    s["eb"][...] = eb_ref[...].astype(f32).reshape(1, LW)
     post = post_ref[...].astype(f32)
     dbias = db_ref[...].astype(f32)
     half = pl.ds(pl.multiple_of(m * HL, HL), HL)
@@ -215,7 +222,7 @@
 
     def mp_and_tp_sum(b, t, left, weight):
         s["ms"][t, b] = dot(left, weight[:, other]).astype(bf16)
-        c = send(s["ms"].at[t, b], s["mr"].at[t, b], to_m)
+        c = send([(s["ms"].at[t, b], s["mr"].at[t, b], to_m)], s["mr"].at[t, b])
         mine = dot(left, weight[:, half])
         c.wait_recv()
         both = mine + s["mr"][t, b].astype(f32)
@@ -243,7 +250,7 @@
         yield
         wait(c)
         s["hs"][0, b] = total(s["pm"][0, b, q], s["rm"].at[0, b], 16).astype(bf16)
-        c = [send(s["hs"].at[0, b], s["hr"].at[0, b], to_h)]
+        c = send([(s["hs"].at[0, b], s["hr"].at[0, b], to_h)], s["hr"].at[0, b])
         yield
         wait(c)
         mixed = s["hs"][0, b].astype(f32) + s["hr"][0, b].astype(f32)
@@ -260,12 +267,12 @@
         yield
         wait(c)
         yield from mp_and_tp_sum(b, 0, merge(s["rsd"][b], R), ew_ref)
-        pre_act = z_total(s["pe"][0, b, i], s["re"].at[0, b]) + eb_ref[:, half].astype(f32)
+        pre_act = z_total(s["pe"][0, b, i], s["re"].at[0, b]) + s["eb"][:, half]
         active = jnp.maximum(pre_act, 0.0)
         s["act"][b] = active
         s["fe"][b, m, i] = (active * active).astype(bf16)
         yield from z_gather(s["fe"].at[b, m])
-        c = [send(s["fe"].at[b, m], s["fe"].at[b, m], to_m)]
+        c = send([(s["fe"].at[b, m], s["fe"].at[b, m], to_m)], s["fe"].at[b, 0])
         yield
         wait(c)
         recon = dot(merge(s["fe"][b, 0], R), dw_ref[:, :HL], LAST)
@@ -274,7 +281,7 @@
         yield
         wait(c)
         s["hs"][1, b] = total(s["pm"][1, b, q], s["rm"].at[1, b], 16).astype(bf16)
-        c = [send(s["hs"].at[1, b], s["hr"].at[1, b], to_h)]
+        c = send([(s["hs"].at[1, b], s["hr"].at[1, b], to_h)], s["hr"].at[1, b])
         yield
         wait(c)
         error = s["hs"][1, b].astype(f32) + s["hr"][1, b].astype(f32) + dbias - s["rsd"][b, q].astype(f32)
@@ -288,7 +295,7 @@
         grad = z_total(s["pe"][1, b, i], s["re"].at[1, b]) + s["wrow"][own_z, :][:, :1] * norm_total
         s["pd"][b, m, i] = (grad * 2.0 * s["act"][b]).astype(bf16)
         yield from z_gather(s["pd"].at[b, m])
-        c = [send(s["pd"].at[b, m], s["pd"].at[b, m], to_m)]
+        c = send([(s["pd"].at[b, m], s["pd"].at[b, m], to_m)], s["pd"].at[b, 0])
         yield
         wait(c)
 
@@ -297,7 +304,7 @@
     running = [(b, block(b)) for b in range(NB)]
     phase = 0
     while running:
-        running = [(b, g) for b, g in running if phase < b * LAG or next(g, True) is None]
+        running = [(b, g) for b, g in running if next(g, True) is None]
         phase += 1
         if phase == 2:
             wait(norm_copies)
@@ -305,7 +312,7 @@
             for k in range(1, 8):
                 squares = squares + s["nsq"][k]
             s["cn"][m] = jnp.sqrt(squares + EPS)
-            cn_copy = send(s["cn"].at[m], s["cn"].at[m], to_m)
+            cn_copy = send([(s["cn"].at[m], s["cn"].at[m], to_m)], s["cn"].at[0])
         if phase == 3:
             cn_copy.wait_recv()
         if len(known) == NB:
@@ -333,9 +340,6 @@
 
 
 def local(*args):
-    args = list(args)
-    for n in (7, 10, 11, 12):
-        args[n] = args[n][None]
     vmem = pl.BlockSpec(memory_space=pltpu.VMEM)
     any_ = pl.BlockSpec(memory_space=pl.ANY)
     out = jax.ShapeDtypeStruct((1, CW, LW), bf16)

time: 178 us -> 166 us (0.933)
  Pallas kernels: 172 us -> 162 us
  local copies, waits for them, and re-layouts: 5.7 us -> 3.17 us
    pallas_call x1, Pallas kernels: 172 us -> 162 us  [local(): pl.pallas_call(kernel, out_shape=(out, out), in_specs=[any_ if n in (2, 3...]
    broadcast_in_dim x3 -> x0, local copies, waits for them, and re-layouts: 2.43 us -> none  [local(): args[n] = args[n][None]]
where the time goes in v3:
time: 166 us
  Pallas kernels  162 us (98%)
  local copies, waits for them, and re-layouts  3.17 us (2%)
    pallas_call x1, Pallas kernels, local(): pl.pallas_call(kernel, out_shape=(out, out), in_specs=[any_ if n in (2, 3...  162 us

profile of v3, /device:TPU:1, one launch (start us, length us, event | category | flops | bytes accessed | tf_op | source)
XLA Modules:
  0.0 165.5 jit_solution(9119102707061281556)
XLA Ops:
  0.6 161.7 %shard_map.140 = (bf16[1,448,1024]{2,1,0:T(8,128)(2,1)}, bf16[1,448,1024]{2,1,0:T(8,128)(2,1)}) custom-call(bf16[1,12,3584]{2,1,0:T(8,128)(2,1)} %refs_0_.1, bf16[1,3584]{1,0:T(2,128)(2,1)} %refs_1_.1, bf16[1,448,448]{2,1,0:T(8,128)(2,1)} %refs_2_.1, bf16[1,448,448]{2,1,0:T(8,128)(2,1)} %refs_3_.1, bf16[1,448,448]{2,1,0:T(8,128)(2,1)} %refs_4_.1, ...), custom_call_target="tpu_custom_call" | custom-call | flops 2300000000 | bytes 7000000 | tf_op jit(solution)/shard_map/pallas_call | solution.py:346
  162.4 0.0 copy-start
  162.4 2.2 %copy.17 = bf16[1,448,1024]{2,1,0:T(8,128)(2,1)} copy(bf16[1,448,1024]{2,1,0:T(8,128)(2,1)} %get-tuple-element.4) | data formatting | bytes 1835008
  164.6 0.0 copy-done
  164.6 0.9 copy.18
Async XLA Ops:
  162.4 2.3 %copy-start = (bf16[1,448,1024]{2,1,0:T(8,128)(2,1)S(1)}, bf16[1,448,1024]{2,1,0:T(8,128)(2,1)}, u32[]{:S(2)}) copy-start(bf16[1,448,1024]{2,1,0:T(8,128)(2,1)} %get-tuple-element.5) | copy-start | bytes 2752516

commit v4 on v3

--- a/solution.py
+++ b/solution.py
@@ -33,9 +33,8 @@
 
 
 SCRATCH = {
-    "payload": pltpu.VMEM((2, 12, 512), bf16),
-    "own24": pltpu.VMEM((24, 512), f32),
-    "nx": pltpu.VMEM((16, 24, 512), bf16),
+    "edge": pltpu.VMEM((4, 12, 512), bf16),
+    "nx": pltpu.VMEM((2, 16, 12, 512), bf16),
     "xf": pltpu.VMEM((ROWS, 512), f32),
     "wgu": pltpu.VMEM((2 * CW, CW), bf16),
     "wrow": pltpu.VMEM((ROWS, 128), f32),
@@ -65,7 +64,7 @@
     "dg": pltpu.VMEM((CW, LW), bf16),
     "eb": pltpu.VMEM((1, LW), f32),
     "load": pltpu.SemaphoreType.DMA((8,)),
-    "sem": pltpu.SemaphoreType.DMA((2, 32 * NB + 4)),
+    "sem": pltpu.SemaphoreType.DMA((2, 32 * NB + 6)),
 }
 
 
@@ -84,7 +83,10 @@
     to_m = {"mp": 1 - m}
 
     gate = pltpu.get_barrier_semaphore()
-    everyone = to_z + to_xy + [to_h, to_m]
+    other_lat = 2 * q + 1 - h
+    nearest = {"tp": jnp.where(i < 4, 7, 0), "lat": other_lat}
+    at_edge = jnp.logical_or(i == 0, i == 7)
+    everyone = to_z + to_xy + [to_h, to_m, nearest]
     for d in everyone:
         pl.semaphore_signal(gate, inc=1, device_id=d, device_id_type=MESH)
 
@@ -125,13 +127,13 @@
     def z_scatter(src, dst):
         far = send([(src.at[4 - 4 * side + p], dst.at[k], to_mate[k - 1])
                     for k, p in enumerate(mates, 1)], dst.at[pl.ds(1, 3)])
-        near = send([(src.at[4 * side + p], dst.at[4 + k], to_mate[k - 1])
-                     for k, p in enumerate(mates, 1)], dst.at[pl.ds(5, 3)])
         yield
         wait(far)
         src[across] = (src[across].astype(f32) + dst[1].astype(f32)
                        + dst[2].astype(f32) + dst[3].astype(f32)).astype(bf16)
         last = send([(src.at[across], dst.at[4], to_across)], dst.at[4])
+        near = send([(src.at[4 * side + p], dst.at[4 + k], to_mate[k - 1])
+                     for k, p in enumerate(mates, 1)], dst.at[pl.ds(5, 3)])
         yield
         wait(near, last)
 
@@ -171,28 +173,45 @@
     p0 = scale.astype(bf16).astype(f32)
     p1 = (scale - p0).astype(bf16).astype(f32)
     p2 = scale - p0 - p1
+    lane = lax.broadcasted_iota(jnp.int32, (12, 512), 1)
+
+    def payload(cols):
+        wide = jnp.concatenate([cols, jnp.zeros((12, 64), f32)], axis=1)
+        wide = jnp.where(lane == CW, p0, jnp.where(lane == CW + 1, p1, jnp.where(lane == CW + 2, p2, wide)))
+        return wide.astype(bf16)
+
     cols = jnp.zeros((12, CW), f32)
     gain_in = jnp.zeros((1, CW), f32)
     pre = pre_ref[...].astype(f32)
     for c in range(8):
         cols = jnp.where(i == c, x[:, c * CW:(c + 1) * CW], cols)
         gain_in = jnp.where(i == c, pre[:, c * CW:(c + 1) * CW], gain_in)
-    payload = jnp.concatenate([cols, jnp.zeros((12, 64), f32)], axis=1)
-    lane = lax.broadcasted_iota(jnp.int32, (12, 512), 1)
-    payload = jnp.where(lane == CW, p0, jnp.where(lane == CW + 1, p1, jnp.where(lane == CW + 2, p2, payload)))
-    s["payload"][h] = payload.astype(bf16)
-
-    pl.semaphore_wait(gate, len(everyone))
-
-    first = send([(s["payload"].at[h], s["payload"].at[h], to_h)], s["payload"].at[0])
+    s["nx"][h, q] = payload(cols)
+    for edge, low in ((7, 0), (0, 4)):
+        @pl.when(i == edge)
+        def _():
+            for c in range(4):
+                s["edge"][c] = payload(x[:, (low + c) * CW:(low + c + 1) * CW])
+
+    pl.semaphore_wait(gate, jnp.where(at_edge, len(everyone) + 3, len(everyone) - 1))
+
+    edge_n = used[0]
+    used[0] += 1
+    for edge, low in ((7, 0), (0, 4)):
+        @pl.when(i == edge)
+        def _():
+            for c in range(4):
+                link(edge_n, s["edge"].at[c], s["nx"].at[h, q], {"tp": low + c, "lat": other_lat}).start()
+
+    def rows_gather(part):
+        return send([(part.at[q], part.at[q], d) for d in to_xy], part.at[pl.ds(0, 15)])
+
+    own_copies = rows_gather(s["nx"].at[h])
     load_d.wait()
     dw = dw_ref[...].astype(f32)
     s["nsq"][i] = jnp.sum(dw * dw, axis=0, keepdims=True)
-    wait(first)
-    s["own24"][0:12] = s["payload"][0].astype(f32)
-    s["own24"][12:24] = s["payload"][1].astype(f32)
-    s["nx"][q] = s["own24"][...].astype(bf16)
-    x_copies = xy_gather(s["nx"])
+    link(edge_n, s["nx"].at[0, 0], s["nx"].at[0, 0], to_m).wait_recv()
+    other_copies = rows_gather(s["nx"].at[1 - h])
     norm_copies = z_share(s["nsq"])
 
     def column(v):
@@ -217,8 +236,9 @@
 
     for c in load_g + load_w:
         c.wait()
-    wait(x_copies)
-    s["xf"][...] = s["nx"][...].astype(f32).reshape(ROWS, 512)
+    wait(own_copies, other_copies)
+    for c in range(32):
+        s["xf"][12 * c:12 * (c + 1)] = s["nx"][c % 2, c // 2].astype(f32)
 
     def mp_and_tp_sum(b, t, left, weight):
         s["ms"][t, b] = dot(left, weight[:, other]).astype(bf16)
@@ -335,6 +355,11 @@
         out_copies.append(local_copy(eg_ref.at[:, at], eg_hbm.at[0, :, at], 6 + p))
     for c in sends:
         c.wait_send()
+
+    @pl.when(at_edge)
+    def _():
+        link(edge_n, s["edge"], s["edge"], to_m).wait_send()
+
     for c in out_copies:
         c.wait()
 

time: 166 us -> 161 us (0.970)
  Pallas kernels: 162 us -> 157 us
    pallas_call x1, Pallas kernels: 162 us -> 157 us  [local(): pl.pallas_call(kernel, out_shape=(out, out), in_specs=[any_ if n in (2, 3...]
where the time goes in v4:
time: 161 us
  Pallas kernels  157 us (98%)
  local copies, waits for them, and re-layouts  3.17 us (2%)
    pallas_call x1, Pallas kernels, local(): pl.pallas_call(kernel, out_shape=(out, out), in_specs=[any_ if n in (2, 3...  157 us

profile of v4, /device:TPU:1, one launch (start us, length us, event | category | flops | bytes accessed | tf_op | source)
XLA Modules:
  0.0 161.0 jit_solution(16410783396653811484)
XLA Ops:
  0.6 157.2 %shard_map.140 = (bf16[1,448,1024]{2,1,0:T(8,128)(2,1)}, bf16[1,448,1024]{2,1,0:T(8,128)(2,1)}) custom-call(bf16[1,12,3584]{2,1,0:T(8,128)(2,1)} %refs_0_.1, bf16[1,3584]{1,0:T(2,128)(2,1)} %refs_1_.1, bf16[1,448,448]{2,1,0:T(8,128)(2,1)} %refs_2_.1, bf16[1,448,448]{2,1,0:T(8,128)(2,1)} %refs_3_.1, bf16[1,448,448]{2,1,0:T(8,128)(2,1)} %refs_4_.1, ...), custom_call_target="tpu_custom_call" | custom-call | flops 2300000000 | bytes 7000000 | tf_op jit(solution)/shard_map/pallas_call | solution.py:371
  157.9 0.0 copy-start
  157.9 2.2 %copy.17 = bf16[1,448,1024]{2,1,0:T(8,128)(2,1)} copy(bf16[1,448,1024]{2,1,0:T(8,128)(2,1)} %get-tuple-element.4) | data formatting | bytes 1835008
  160.1 0.0 copy-done
  160.1 0.9 copy.18
Async XLA Ops:
  157.9 2.3 %copy-start = (bf16[1,448,1024]{2,1,0:T(8,128)(2,1)S(1)}, bf16[1,448,1024]{2,1,0:T(8,128)(2,1)}, u32[]{:S(2)}) copy-start(bf16[1,448,1024]{2,1,0:T(8,128)(2,1)} %get-tuple-element.5) | copy-start | bytes 2752516

commit v5 on v4

--- a/solution.py
+++ b/solution.py
@@ -244,6 +244,7 @@
         s["ms"][t, b] = dot(left, weight[:, other]).astype(bf16)
         c = send([(s["ms"].at[t, b], s["mr"].at[t, b], to_m)], s["mr"].at[t, b])
         mine = dot(left, weight[:, half])
+        yield
         c.wait_recv()
         both = mine + s["mr"][t, b].astype(f32)
         s["pe"][t, b] = both.reshape(8, RZ, HL).astype(bf16)

time: 161 us -> 164 us (1.019)
  Pallas kernels: 157 us -> 160 us
    pallas_call x1, Pallas kernels: 157 us -> 160 us  [local(): pl.pallas_call(kernel, out_shape=(out, out), in_specs=[any_ if n in (2, 3...]
where the time goes in v5:
time: 164 us
  Pallas kernels  160 us (98%)
  local copies, waits for them, and re-layouts  3.17 us (2%)
    pallas_call x1, Pallas kernels, local(): pl.pallas_call(kernel, out_shape=(out, out), in_specs=[any_ if n in (2, 3...  160 us

profile of v5, /device:TPU:1, one launch (start us, length us, event | category | flops | bytes accessed | tf_op | source)
XLA Modules:
  0.0 163.7 jit_solution(1182572980784060291)
XLA Ops:
  0.6 159.9 %shard_map.140 = (bf16[1,448,1024]{2,1,0:T(8,128)(2,1)}, bf16[1,448,1024]{2,1,0:T(8,128)(2,1)}) custom-call(bf16[1,12,3584]{2,1,0:T(8,128)(2,1)} %refs_0_.1, bf16[1,3584]{1,0:T(2,128)(2,1)} %refs_1_.1, bf16[1,448,448]{2,1,0:T(8,128)(2,1)} %refs_2_.1, bf16[1,448,448]{2,1,0:T(8,128)(2,1)} %refs_3_.1, bf16[1,448,448]{2,1,0:T(8,128)(2,1)} %refs_4_.1, ...), custom_call_target="tpu_custom_call" | custom-call | flops 2300000000 | bytes 7000000 | tf_op jit(solution)/shard_map/pallas_call | solution.py:372
  160.6 0.0 copy-start
  160.6 2.2 %copy.17 = bf16[1,448,1024]{2,1,0:T(8,128)(2,1)} copy(bf16[1,448,1024]{2,1,0:T(8,128)(2,1)} %get-tuple-element.4) | data formatting | bytes 1835008
  162.8 0.0 copy-done
  162.8 0.9 copy.18
Async XLA Ops:
  160.6 2.3 %copy-start = (bf16[1,448,1024]{2,1,0:T(8,128)(2,1)S(1)}, bf16[1,448,1024]{2,1,0:T(8,128)(2,1)}, u32[]{:S(2)}) copy-start(bf16[1,448,1024]{2,1,0:T(8,128)(2,1)} %get-tuple-element.5) | copy-start | bytes 2752516
